TPU v7x, 32 devices: a whole 2x2x4 slice. The times are simulated.
32 devices in a mesh: group: 2 (over y), shard: 16 (over z, x, core).
Axes of the slice: x: 2, y: 2, z: 4, core: 2. Of those that a mesh axis runs over, the one named last changes fastest.
Arguments:
- gradients: bfloat16 [2, 16, 256, 8192], P('group', 'shard'), may hold values from -1.59375 to 1.59375
- momentum: float32 [2, 256, 8192], P('group', None, 'shard'), may hold values from -6 to 6
- master: float32 [256, 8192], P(None, 'shard'), may hold values from -0.6 to 0.6
- indices: int32 [2, 4, 128, 32], P('group', None, 'shard'), may hold values from 0 to 4095, as said below
Outputs:
- momentum_out: float32 [2, 256, 8192], P('group', None, 'shard')
- master_out: float32 [256, 8192], P(None, 'shard')
- params_full: bfloat16 [256, 8192], replicated
Inputs may be any that keep to these rules, and one draw needn't show every extreme that they name: `indices`: the 32 positions of one group and block are distinct.
All inputs are finite; a program needn't handle non-finite values.
Results may differ from a plain program's by a relative error of at most 0.001.
Values may be sent and summed in bfloat16 or wider, within the bound.
A program may use at most 128 MiB of HBM per device.

v0:
```python
import jax
import jax.numpy as jnp
from jax import lax
from jax.sharding import PartitionSpec as P

BLOCK = 64


momentum_decay = 0.9
step_rate = 0.5


def cosine_table(side):
    freqs = jnp.arange(side, dtype=jnp.float32)[:, None]
    places = jnp.arange(side, dtype=jnp.float32)[None, :]
    table = jnp.cos(jnp.pi * (2.0 * places + 1.0) * freqs / (2.0 * side))
    weights = jnp.where(freqs == 0.0, jnp.sqrt(1.0 / side), jnp.sqrt(2.0 / side))
    return table * weights


def into_blocks(field, side):
    leading = field.shape[:-2]
    depth = len(leading)
    shaped = field.reshape(leading + (field.shape[-2] // side, side, field.shape[-1] // side, side))
    return jnp.moveaxis(shaped, depth + 2, depth + 1)


def out_blocks(blocks):
    leading = blocks.shape[:-4]
    depth = len(leading)
    moved = jnp.moveaxis(blocks, depth + 1, depth + 2)
    return moved.reshape(
        leading + (blocks.shape[-4] * blocks.shape[-2], blocks.shape[-3] * blocks.shape[-1])
    )


def forward_blocks(blocks, table):
    return jnp.einsum("kn,...nm,lm->...kl", table, blocks, table, precision=lax.Precision.HIGHEST)


def inverse_blocks(blocks, table):
    return jnp.einsum("kn,...kl,lm->...nm", table, blocks, table, precision=lax.Precision.HIGHEST)


def scatter_picked(picked, positions, target_shape):
    places = [
        lax.broadcasted_iota(jnp.int32, positions.shape, dimension)
        for dimension in range(positions.ndim - 1)
    ]
    return jnp.zeros(target_shape, picked.dtype).at[tuple(places) + (positions,)].add(picked)


def local(gradients, momentum, master, indices):
    table = cosine_table(BLOCK)
    height = master.shape[0] // BLOCK
    across = master.shape[1] // BLOCK
    local_ids = indices[0]
    local_grad = gradients[0, 0]
    summed = lax.psum_scatter(
        local_grad.astype(jnp.float32), "shard", scatter_dimension=1, tiled=True
    )
    accumulated = momentum_decay * momentum[0] + summed
    coeffs = forward_blocks(into_blocks(accumulated, BLOCK), table)
    flat = coeffs.reshape(height, across, BLOCK * BLOCK)
    picked = jnp.take_along_axis(flat, local_ids, axis=2)
    own_dense = scatter_picked(picked, local_ids, flat.shape)
    momentum_out = accumulated - out_blocks(inverse_blocks(own_dense.reshape(coeffs.shape), table))
    piece_values = lax.all_gather(picked[None], "group", axis=0, tiled=True)
    piece_ids = lax.all_gather(local_ids[None], "group", axis=0, tiled=True)
    piece_ids = piece_ids.astype(jnp.int32)
    first = lax.broadcasted_iota(jnp.int32, piece_ids.shape, 1)
    second = lax.broadcasted_iota(jnp.int32, piece_ids.shape, 2)
    union_sum = jnp.zeros(flat.shape, jnp.float32).at[first, second, piece_ids].add(piece_values)
    change_field = out_blocks(inverse_blocks(union_sum.reshape(coeffs.shape), table))
    master_out = master - step_rate * jnp.tanh(change_field)
    params_full = lax.all_gather(master_out.astype(jnp.bfloat16), "shard", axis=1, tiled=True)
    return (momentum_out[None], master_out, params_full)


def solution(mesh):
    placed = (
        P("group", "shard", None, None),
        P("group", None, "shard"),
        P(None, "shard"),
        P("group", None, "shard", None),
    )
    return jax.shard_map(
        local,
        mesh=mesh,
        in_specs=placed,
        out_specs=(P("group", None, "shard"), P(None, "shard"), P()),
        check_vma=False,
    )
```

profile of v0, /device:TPU:0, one launch (start us, length us, event | category | flops | bytes accessed | tf_op | source)
XLA Modules:
  0.0 221.0 jit_solution(11557623136489242930)
XLA Ops:
  7.2 6.4 %bitcast_convert_fusion = f32[256,8192]{1,0:T(8,128)} fusion(bf16[1,1,256,8192]{3,2,1,0:T(8,128)(2,1)} %param.4), kind=kLoop, calls=%fused_computation.3 | loop fusion | flops 2097152 | bytes 12582912 | tf_op jit(solution)/shard_map/convert_element_type | solution.py:60
  13.7 0.6 copy-done.2
  14.3 5.3 %all_gather.9 = s32[2,4,8,32]{3,2,1,0:T(8,128)S(1)} all-gather(s32[1,4,8,32]{3,2,1,0:T(8,128)S(1)} %copy-done.2), channel_id=1, replica_groups=mesh['group'=2,'shard'=16] {'group'}, dimensions={0}, use_global_device_ids=true | all-gather | bytes 12288 | tf_op jit(solution)/shard_map/all_gather | solution.py:69
  20.1 101.3 %reduce-scatter.2.cloned.1.call-done = f32[256,512]{1,0:T(8,128)} async-done(((f32[256,8192]{1,0:T(8,128)}), f32[256,512]{1,0:T(8,128)}) %reduce-scatter.2.cloned.1.call-update) | async-done | bytes 524304 | tf_op jit(solution)/shard_map/reduce_scatter | solution.py:59
  121.4 1.1 bitcast_add_fusion
  122.7 0.4 copy.15
  123.1 3.2 %fusion.2 = f32[4,8,64,64]{2,3,1,0:T(8,128)S(1)} fusion(f32[4,64,8,64]{1,3,2,0:T(8,128)S(1)} %copy.15, f32[64]{0:T(128)S(1)} %get-tuple-element.7, f32[64]{0:T(128)S(1)} %get-tuple-element.8), kind=kOutput, calls=%fused_computation.8 | convolution fusion | flops 100675584 | bytes 1049088 | tf_op jit(solution)/shard_map/kn,...nm,lm->...kl/dot_general | solution.py:38
  126.2 1.1 fusion.15
  127.3 0.4 reshape.83
  127.7 8.4 %gather_fusion = f32[1024]{0:T(1024)S(1)} fusion(f32[4,8,4096]{2,1,0:T(8,128)S(1)} %reshape.83, s32[1024]{0:T(1024)S(1)} %reshape.98), kind=kCustom, calls=%fused_computation | custom fusion | bytes 20480 | tf_op jit(solution)/shard_map/jit(take_along_axis)/gather | solution.py:65
  136.2 4.4 %all_gather.10 = f32[2,4,8,32]{3,2,1,0:T(8,128)S(1)} all-gather(f32[1,4,8,32]{3,2,1,0:T(8,128)S(1)} %and_select_fusion), channel_id=1, replica_groups=mesh['group'=2,'shard'=16] {'group'}, dimensions={0}, use_global_device_ids=true | all-gather | bytes 12288 | tf_op jit(solution)/shard_map/all_gather | solution.py:68
  140.7 11.4 %scatter_custom_fusion.1 = f32[131072]{0:T(1024)S(1)} fusion(s32[2048]{0:T(1024)S(1)} %reshape.110, f32[2048]{0:T(1024)S(1)} %reshape.112, f32[]{:T(128)} %constant.16.clone.1), kind=kCustom, calls=%fused_computation.12 | custom fusion | flops 2048 | bytes 524292
  152.3 1.2 fusion.10
  153.4 1.1 fusion.1
  154.5 0.6 copy.22
  155.2 0.3 mul.149
  155.4 1.0 fusion.42
  156.9 6.2 %scatter_custom_fusion = f32[131072]{0:T(1024)S(1)} fusion(s32[1024]{0:T(1024)S(1)} %reshape.104, f32[1024]{0:T(1024)S(1)} %reshape.106, f32[]{:T(128)} %constant.16.clone.1), kind=kCustom, calls=%fused_computation.14 | custom fusion | flops 1024 | bytes 524292
  163.3 1.2 fusion.13
  164.5 1.1 convolution_bitcast_fusion
  165.6 0.6 copy.19
  166.5 0.9 subtract_bitcast_fusion
  167.4 42.2 %all-gather.2.cloned.1.call-done = bf16[256,8192]{1,0:T(8,128)(2,1)} async-done(((bf16[256,512]{1,0:T(8,128)(2,1)}), bf16[256,8192]{1,0:T(8,128)(2,1)}) %all-gather.2.cloned.1.call-update) | async-done | bytes 4194320 | tf_op jit(solution)/shard_map/all_gather | solution.py:76
  209.6 4.6 %copy.30 = bf16[256,8192]{1,0:T(8,128)(2,1)} copy(bf16[256,8192]{1,0:T(8,128)(2,1)} %all-gather.2.cloned.1.call-done) | data formatting | bytes 8388608
  (39 shorter events, 1.9 us)
Async XLA Ops:
  7.2 114.2 %reduce-scatter.2.cloned.1.call-start = ((), (), s32[]{:S(2)}) async-start(), calls=%async_computation.1 | async-start | bytes 8912896 | tf_op jit(solution)/shard_map/reduce_scatter | solution.py:59
  13.6 0.7 copy-start.2
  13.6 6.1 %copy-start.3 = (s32[3]{0:T(128)S(1)}, s32[3]{0:T(128)}, u32[]{:S(2)}) copy-start(s32[3]{0:T(128)} %constant.55) | copy-start | bytes 40
  13.6 6.2 %copy-start.4 = (s32[3]{0:T(128)S(1)}, s32[3]{0:T(128)}, u32[]{:S(2)}) copy-start(s32[3]{0:T(128)} %constant.58) | copy-start | bytes 40
  13.6 107.7 %copy-start = (f32[1,256,512]{2,1,0:T(8,128)S(1)}, f32[1,256,512]{2,1,0:T(8,128)}, u32[]{:S(2)}) copy-start(f32[1,256,512]{2,1,0:T(8,128)} %param.5) | copy-start | bytes 1572868
  13.7 195.9 %all-gather.2.cloned.1.call-start = ((), (), s32[]{:S(2)}) async-start(), calls=%async_computation.2 | async-start | bytes 4456448 | tf_op jit(solution)/shard_map/all_gather | solution.py:76
  152.3 3.2 %copy-start.1 = (f32[256,512]{1,0:T(8,128)S(1)}, f32[256,512]{1,0:T(8,128)}, u32[]{:S(2)}) copy-start(f32[256,512]{1,0:T(8,128)} %param.6) | copy-start | bytes 1572868
Sparse Core Ops, SparseCore 0:
  13.8 107.5 reduce-scatter.1
  156.6 52.9 all-gather.1
where the time goes:
time: 221 us
  waiting for transfers between devices  144 us (65%)
  other arithmetic  27.4 us (12%)
  local copies, waits for them, and re-layouts  17.3 us (8%)
  between operations  14.3 us (6%)
  blocking collectives  9.73 us (4%)
  matrix products  8.77 us (4%)
    reduce_scatter x1, waiting for transfers between devices, local(): lax.psum_scatter(local_grad.astype(jnp.float32), 'shard', scatter_dimensi...  101 us
    all_gather x1, waiting for transfers between devices, local(): lax.all_gather(master_out.astype(jnp.bfloat16), 'shard', axis=1, tiled=True)  42.2 us
    unnamed x8, other arithmetic  18 us
    gather x3, local copies, waits for them, and re-layouts, local(): picked = jnp.take_along_axis(flat, local_ids, axis=2)  8.53 us
    convert_element_type x1, other arithmetic, local(): local_grad.astype(jnp.float32)  6.41 us
    unnamed x13, local copies, waits for them, and re-layouts  5.43 us
    all_gather x1, blocking collectives, local(): piece_ids = lax.all_gather(local_ids[None], 'group', axis=0, tiled=True)  5.32 us
    dot_general x4, matrix products, inverse_blocks(): jnp.einsum('kn,...kl,lm->...nm', table, blocks, table, precision=lax.Prec...  4.5 us
  transfers between devices with their start and end apart: 2, of which 2 were waited for; matrix products, arithmetic and copies ran while one was open for 5% of the time, Pallas kernels for 0%

commit v1 on v0

v1 whole, which is shorter than its diff:
```python
import functools

import jax
import jax.numpy as jnp
import numpy as np
from jax import lax
from jax.experimental import pallas as pl
from jax.experimental.pallas import tpu as pltpu
from jax.sharding import PartitionSpec as P

BLOCK = 64
LANES = 128
TOP = 32767.0

momentum_decay = 0.9
step_rate = 0.5

HI = lax.Precision.HIGHEST
MESH = pl.DeviceIdType.MESH
F32 = jnp.float32
BF16 = jnp.bfloat16


def cosine_table(side):
    freqs = np.arange(side, dtype=np.float64)[:, None]
    places = np.arange(side, dtype=np.float64)[None, :]
    table = np.cos(np.pi * (2.0 * places + 1.0) * freqs / (2.0 * side))
    weights = np.where(freqs == 0.0, np.sqrt(1.0 / side), np.sqrt(2.0 / side))
    return table * weights


def split3(x):
    high = x.astype(BF16)
    rest = x - high.astype(F32)
    mid = rest.astype(BF16)
    low = (rest - mid.astype(F32)).astype(BF16)
    return high, mid, low


def dot(a, b):
    return jnp.dot(a, b, precision=HI, preferred_element_type=F32)


def dot_nt(a, b, precision=None):
    return lax.dot_general(a, b, (((1,), (1,)), ((), ())), precision=precision, preferred_element_type=F32)


def kernel(n_group, n, width, side,
           grad, mom, master, idx, rt, rtt, ct,
           mom_out, master_out, params_out,
           mine, sib, sendq, recvq, sends, recvs, acc, coefs_t, dense, union, param, idx_all, pick_all,
           mine_sem, raw_send, raw_recv, q_send, q_recv, s_send, s_recv,
           idx_send, idx_recv, pick_send, pick_recv,
           own_sem, ag_send, ag_recv, fw_send, fw_recv):
    rows = master.shape[0]
    half = rows // 2
    height = rows // BLOCK
    steps = n // 2
    count = 2 * steps - 1
    slots = idx.shape[1]
    per_block = slots // (width // BLOCK)

    g = lax.axis_index("group")
    s = lax.axis_index("shard")
    core = lax.rem(s, 2)
    chip = s // 2
    odd = lax.rem(chip, 2)
    pos = (1 - odd) * (chip // 2) + odd * (n - 1 - chip // 2)

    def chip_at(offset):
        place = lax.rem(pos + (offset % n), n)
        back = place // (n // 2)
        return (1 - back) * (2 * place) + back * (2 * (n - 1 - place) + 1)

    sibling = 2 * chip + (1 - core)
    beside = {1: 2 * chip_at(1) + core, -1: 2 * chip_at(-1) + core}

    def columns(shard):
        return pl.ds(pl.multiple_of(shard * width, LANES), width)

    def other_group(k):
        return lax.rem(g + k, n_group)

    barrier = pltpu.get_barrier_semaphore()
    for sign in (1, -1):
        pl.semaphore_signal(barrier, inc=1, device_id={"shard": beside[sign]}, device_id_type=MESH)
    pl.semaphore_signal(barrier, inc=1, device_id={"shard": sibling}, device_id_type=MESH)
    for k in range(1, n_group):
        pl.semaphore_signal(barrier, inc=1, device_id={"group": other_group(k)}, device_id_type=MESH)

    order = [steps]
    for t in range(1, steps):
        order += [steps - t, n - (steps - t)]
    order += [0]

    own_loads = {}
    for r in order:
        own_loads[r] = pltpu.make_async_copy(
            grad.at[0, 0, :, columns(2 * chip_at(r) + core)], mine.at[r], mine_sem.at[r])
        own_loads[r].start()

    pl.semaphore_wait(barrier, 3 + n_group - 1)

    raw = {}
    for r in order:
        raw[r] = pltpu.make_async_remote_copy(
            src_ref=grad.at[0, 0, :, columns(2 * chip_at(r) + 1 - core)], dst_ref=sib.at[r],
            send_sem=raw_send.at[r], recv_sem=raw_recv.at[r],
            device_id={"shard": sibling}, device_id_type=MESH)
        raw[r].start()

    idx_copies = []
    for k in range(1, n_group):
        copy = pltpu.make_async_remote_copy(
            src_ref=idx, dst_ref=idx_all.at[k - 1],
            send_sem=idx_send.at[k - 1], recv_sem=idx_recv.at[k - 1],
            device_id={"group": other_group(k)}, device_id_type=MESH)
        copy.start()
        idx_copies.append(copy)

    def own_first(sign):
        return 0 if sign == 1 else 1

    ready = set()

    def arrived(r):
        if r not in ready:
            ready.add(r)
            own_loads[r].wait()
            raw[r].wait_recv()

    def q_copies(sign, m):
        d = 0 if sign == 1 else 1
        there = {"shard": beside[sign]}
        return (
            pltpu.make_async_remote_copy(
                src_ref=sendq.at[d, m], dst_ref=recvq.at[d, m],
                send_sem=q_send.at[d, m], recv_sem=q_recv.at[d, m],
                device_id=there, device_id_type=MESH),
            pltpu.make_async_remote_copy(
                src_ref=sends.at[d, m], dst_ref=recvs.at[d, m],
                send_sem=s_send.at[d, m], recv_sem=s_recv.at[d, m],
                device_id=there, device_id_type=MESH))

    def message(t, first):
        return 0 if t == 0 else 2 * t - 1 + (1 if first else 0)

    def received(d, m, lane):
        scale = recvs[d, m, 0:1, :]
        return recvq[d, m, :, pl.ds(lane * LANES, LANES)].astype(jnp.int32).astype(F32) * scale

    tiles = width // LANES
    for t in range(steps):
        for first in ((True,) if t == 0 else (False, True)):
            for sign in (1, -1):
                d = 0 if sign == 1 else 1
                part = own_first(sign) if first else 1 - own_first(sign)
                r = (sign * (steps - t)) % n
                m = message(t, first)
                arrived(r)
                has = t >= 2 or (t == 1 and first)
                if has:
                    before = message(t - 1, first)
                    for copy in q_copies(sign, before):
                        copy.wait_recv()
                band = pl.ds(part * half, half)
                values = []
                top = None
                for lane in range(tiles):
                    cols = pl.ds(lane * LANES, LANES)
                    x = mine[r, band, cols].astype(F32) + sib[r, band, cols].astype(F32)
                    if has:
                        x = x + received(d, before, lane)
                    values.append(x)
                    peak = jnp.max(jnp.abs(x), axis=0, keepdims=True)
                    top = peak if top is None else jnp.maximum(top, peak)
                top = jnp.maximum(top, 1e-30)
                inverse = TOP / top
                for lane in range(tiles):
                    q = jnp.round(values[lane] * inverse).astype(jnp.int32).astype(jnp.int16)
                    sendq[d, m, :, pl.ds(lane * LANES, LANES)] = q
                sends[d, m] = jnp.broadcast_to(top * (1.0 / TOP), (8, LANES))
                for copy in q_copies(sign, m):
                    copy.start()

    arrived(0)
    for first in (False, True):
        for sign in (1, -1):
            for copy in q_copies(sign, message(steps - 1, first)):
                copy.wait_recv()
    for part in range(2):
        band = pl.ds(part * half, half)
        for lane in range(tiles):
            cols = pl.ds(lane * LANES, LANES)
            x = mine[0, band, cols].astype(F32) + sib[0, band, cols].astype(F32)
            for sign in (1, -1):
                x = x + received(0 if sign == 1 else 1, message(steps - 1, part == own_first(sign)), lane)
            acc[band, cols] = momentum_decay * mom[0, band, cols] + x

    span = ct.shape[0]
    stage = dot(rt[...], acc[...])
    for tile in range(width // span):
        coefs_t[pl.ds(tile * span, span), :] = dot_nt(ct[...], stage[:, tile * span:(tile + 1) * span], HI)

    lane_block = lax.broadcasted_iota(jnp.int32, (1, slots), 1) // per_block

    def row_hot(ids):
        return lax.broadcasted_iota(jnp.int32, (BLOCK, slots), 0) == (ids >> 6)

    def col_hot(ids):
        places = lane_block * BLOCK + (ids & (BLOCK - 1))
        return lax.broadcasted_iota(jnp.int32, (width, slots), 0) == places

    def spread(ids, picked):
        hot = jnp.where(row_hot(ids), picked, 0.0)
        cols = jnp.where(col_hot(ids), 1.0, 0.0).astype(BF16)
        high, mid, low = split3(hot)
        return dot_nt(high, cols) + (dot_nt(mid, cols) + dot_nt(low, cols))

    high, mid, low = split3(coefs_t[...])
    pick_all[0] = jnp.zeros(pick_all.shape[1:], F32)
    for a in range(height):
        ids = idx[a:a + 1, :]
        hot = lax.broadcasted_iota(jnp.int32, (rows, slots), 0) == (ids >> 6) + a * BLOCK
        hot = jnp.where(hot, 1.0, 0.0).astype(BF16)
        at_row = (jnp.dot(high, hot, preferred_element_type=F32)
                  + (jnp.dot(mid, hot, preferred_element_type=F32)
                     + jnp.dot(low, hot, preferred_element_type=F32)))
        pick_all[0, a:a + 1, :] = jnp.sum(jnp.where(col_hot(ids), at_row, 0.0), axis=0, keepdims=True)

    pick_copies = []
    for k in range(1, n_group):
        copy = pltpu.make_async_remote_copy(
            src_ref=pick_all.at[0], dst_ref=pick_all.at[k],
            send_sem=pick_send.at[k - 1], recv_sem=pick_recv.at[k - 1],
            device_id={"group": other_group(k)}, device_id_type=MESH)
        copy.start()
        pick_copies.append(copy)

    for a in range(height):
        dense[pl.ds(a * BLOCK, BLOCK), :] = spread(idx[a:a + 1, :], pick_all[0, a:a + 1, :])
    union[...] = dense[...]
    for k in range(1, n_group):
        idx_copies[k - 1].wait_recv()
        pick_copies[k - 1].wait_recv()
        for a in range(height):
            band = pl.ds(a * BLOCK, BLOCK)
            union[band, :] = union[band, :] + spread(idx_all[k - 1, a:a + 1, :], pick_all[k, a:a + 1, :])

    def back(field, tile):
        return dot(field[:, tile * span:(tile + 1) * span], ct[...])

    stage = dot(rtt[...], union[...])
    for tile in range(width // span):
        cols = pl.ds(tile * span, span)
        new = master[:, cols] - step_rate * jnp.tanh(back(stage, tile))
        master_out[:, cols] = new
        param[:, cols] = new.astype(BF16)

    def place(offset):
        return columns(2 * chip_at(offset) + core)

    def ag_copy(sign, t, part, m):
        d = 0 if sign == 1 else 1
        band = pl.ds(part * half, half)
        where = params_out.at[band, place(-sign * t)]
        return pltpu.make_async_remote_copy(
            src_ref=param.at[band, :] if t == 0 else where, dst_ref=where,
            send_sem=ag_send.at[d, m], recv_sem=ag_recv.at[d, m],
            device_id={"shard": beside[sign]}, device_id_type=MESH)

    def ag_arrival(sign, t, part, m):
        d = 0 if sign == 1 else 1
        where = params_out.at[pl.ds(part * half, half), place(-sign * (t + 1))]
        return pltpu.make_async_remote_copy(
            src_ref=where, dst_ref=where,
            send_sem=ag_send.at[d, m], recv_sem=ag_recv.at[d, m],
            device_id={"shard": beside[sign]}, device_id_type=MESH)

    def fw_copy(sign, t, part, m, c):
        d = 0 if sign == 1 else 1
        where = params_out.at[pl.ds(part * half, half), columns(2 * chip_at(-sign * (t + 1)) + c)]
        return pltpu.make_async_remote_copy(
            src_ref=where, dst_ref=where,
            send_sem=fw_send.at[d, m], recv_sem=fw_recv.at[d, m],
            device_id={"shard": sibling}, device_id_type=MESH)

    trips = [(t, first) for t in range(steps) for first in ((True, False) if t < steps - 1 else (True,))]
    number = {trip: m for m, trip in enumerate(trips)}

    def part_of(sign, first):
        return own_first(sign) if first else 1 - own_first(sign)

    sent = []

    def go(sign, t, first):
        if (t, first) in number:
            copy = ag_copy(sign, t, part_of(sign, first), number[(t, first)])
            copy.start()
            sent.append(copy)

    for first in (True, False):
        for sign in (1, -1):
            go(sign, 0, first)
    own = pltpu.make_async_copy(param, params_out.at[:, place(0)], own_sem)
    own.start()

    def own_forward(c):
        return pltpu.make_async_remote_copy(
            src_ref=param, dst_ref=params_out.at[:, columns(2 * chip + c)],
            send_sem=fw_send.at[0, count], recv_sem=fw_recv.at[0, count],
            device_id={"shard": sibling}, device_id_type=MESH)

    own_forward(core).start()

    stage = dot(rtt[...], dense[...])
    for tile in range(width // span):
        cols = pl.ds(tile * span, span)
        mom_out[0, :, cols] = acc[:, cols] - back(stage, tile)

    for m, (t, first) in enumerate(trips):
        for sign in (1, -1):
            ag_arrival(sign, t, part_of(sign, first), m).wait_recv()
            go(sign, t + 1, first)
            fw_copy(sign, t, part_of(sign, first), m, core).start()

    for m, (t, first) in enumerate(trips):
        for sign in (1, -1):
            fw_copy(sign, t, part_of(sign, first), m, core).wait_send()
            fw_copy(sign, t, part_of(sign, first), m, 1 - core).wait_recv()
    own_forward(core).wait_send()
    own_forward(1 - core).wait_recv()
    own.wait()
    for copy in sent:
        copy.wait_send()
    for r in order:
        raw[r].wait_send()
    for sign in (1, -1):
        for m in range(count):
            for copy in q_copies(sign, m):
                copy.wait_send()
    for copy in idx_copies + pick_copies:
        copy.wait_send()


def local(n_group, n_shard, gradients, momentum, master, indices):
    rows, width = master.shape
    whole = gradients.shape[3]
    n = n_shard // 2
    steps = n // 2
    count = 2 * steps - 1
    height = rows // BLOCK
    slots = indices.shape[2] * indices.shape[3]
    pad = -(-height // 8) * 8
    idx = jnp.pad(indices[0].reshape(height, slots), ((0, pad - height), (0, 0)))
    span = 256 if width % 256 == 0 else 128
    table = cosine_table(BLOCK)
    rt = np.kron(np.eye(height), table).astype(np.float32)
    ct = np.kron(np.eye(span // BLOCK), table).astype(np.float32)
    others = max(n_group - 1, 1)
    dma = pltpu.SemaphoreType.DMA
    vmem = pl.BlockSpec(memory_space=pltpu.VMEM)
    hbm = pl.BlockSpec(memory_space=pl.ANY)
    body = functools.partial(kernel, n_group, n, width, 0)
    return pl.pallas_call(
        body,
        out_shape=(
            jax.ShapeDtypeStruct((1, rows, width), F32),
            jax.ShapeDtypeStruct((rows, width), F32),
            jax.ShapeDtypeStruct((rows, whole), BF16),
        ),
        in_specs=[hbm] + [vmem] * 6,
        out_specs=(vmem, vmem, hbm),
        scratch_shapes=[
            pltpu.VMEM((n, rows, width), BF16),
            pltpu.VMEM((n, rows, width), BF16),
            pltpu.VMEM((2, count, rows // 2, width), jnp.int16),
            pltpu.VMEM((2, count, rows // 2, width), jnp.int16),
            pltpu.VMEM((2, count, 8, LANES), F32),
            pltpu.VMEM((2, count, 8, LANES), F32),
            pltpu.VMEM((rows, width), F32),
            pltpu.VMEM((width, rows), F32),
            pltpu.VMEM((rows, width), F32),
            pltpu.VMEM((rows, width), F32),
            pltpu.VMEM((rows, width), BF16),
            pltpu.VMEM((others, pad, slots), jnp.int32),
            pltpu.VMEM((n_group, pad, slots), F32),
            dma((n,)), dma((n,)), dma((n,)),
            dma((2, count)), dma((2, count)), dma((2, count)), dma((2, count)),
            dma((others,)), dma((others,)), dma((others,)), dma((others,)),
            dma, dma((2, count)), dma((2, count)), dma((2, count + 1)), dma((2, count + 1)),
        ],
        compiler_params=pltpu.CompilerParams(
            collective_id=0, has_side_effects=True, vmem_limit_bytes=44 * 1024 * 1024),
        cost_estimate=pl.CostEstimate(
            flops=30 * rows * rows * width, bytes_accessed=4 * rows * whole, transcendentals=rows * width),
    )(gradients, momentum, master, idx, jnp.asarray(rt), jnp.asarray(rt.T.copy()), jnp.asarray(ct))


def solution(mesh):
    placed = (
        P("group", "shard", None, None),
        P("group", None, "shard"),
        P(None, "shard"),
        P("group", None, "shard", None),
    )
    return jax.shard_map(
        functools.partial(local, mesh.shape["group"], mesh.shape["shard"]),
        mesh=mesh,
        in_specs=placed,
        out_specs=(P("group", None, "shard"), P(None, "shard"), P()),
        check_vma=False,
    )
```

time: 221 us -> 68.2 us (0.31)
  waiting for transfers between devices: 144 us -> 0 us
  Pallas kernels: 0 us -> 58.9 us
  other arithmetic: 27.4 us -> 0 us
  between operations: 14.3 us -> 0.64 us
  blocking collectives: 9.73 us -> 0 us
  local copies, waits for them, and re-layouts: 17.3 us -> 8.39 us
  matrix products: 8.77 us -> 0 us
    reduce_scatter x1 -> x0, waiting for transfers between devices: 101 us -> none  [local(): lax.psum_scatter(local_grad.astype(jnp.float32), 'shard', scatter_dimensi...]
    pallas_call x0 -> x1, Pallas kernels: none -> 58.9 us  [local(): pl.pallas_call(body, out_shape=(jax.ShapeDtypeStruct((1, rows, width), F3...]
    all_gather x1 -> x0, waiting for transfers between devices: 42.2 us -> none  [local(): lax.all_gather(master_out.astype(jnp.bfloat16), 'shard', axis=1, tiled=True)]
    unnamed x8 -> x0, other arithmetic: 18 us -> none
    all_gather x2 -> x0, blocking collectives: 9.73 us -> none  [the longest x1 5.32 us: local(): piece_ids = lax.all_gather(local_ids[None], 'group', axis=0, tiled=True)]
    dot_general x6 -> x0, matrix products: 8.77 us -> none  [the longest x4 4.5 us: inverse_blocks(): jnp.einsum('kn,...kl,lm->...nm', table, blocks, table, precision=lax.Prec...]
    gather x3 -> x0, local copies, waits for them, and re-layouts: 8.53 us -> none  [local(): picked = jnp.take_along_axis(flat, local_ids, axis=2)]
    convert_element_type x2 -> x0, other arithmetic: 7.38 us -> none  [the longest x1 6.41 us: local(): local_grad.astype(jnp.float32)]
  transfers between devices with their start and end apart: 2 -> 0, of which waited for: 2 -> 0; matrix products, arithmetic and copies ran while one was open for 5% -> 0% of each run, Pallas kernels for 0% -> 0%
where the time goes in v1:
time: 68.2 us; the launch traced here: 67.9 us
  Pallas kernels  58.9 us (86%)
  local copies, waits for them, and re-layouts  8.39 us (12%)
    pallas_call x1, Pallas kernels, local(): pl.pallas_call(body, out_shape=(jax.ShapeDtypeStruct((1, rows, width), F3...  58.9 us
    unnamed x11, local copies, waits for them, and re-layouts  7.58 us

profile of v1, /device:TPU:0, one launch (start us, length us, event | category | flops | bytes accessed | tf_op | source)
XLA Modules:
  0.0 67.9 jit_solution(5838764249820504565)
XLA Ops:
  0.6 0.8 %reshape_squeeze.3 = s32[4,256]{1,0:T(4,128)S(1)} reshape(s32[1,4,8,32]{3,2,1,0:T(8,128)} %param.10) | data formatting | bytes 8192 | tf_op jit(solution)/shard_map/reshape;squeeze | solution.py:355
  1.4 0.0 copy-start
  1.4 0.9 %copy-done = f32[256,256]{1,0:T(8,128)S(1)} copy-done((f32[256,256]{1,0:T(8,128)S(1)}, f32[256,256]{1,0:T(8,128)}, u32[]{:S(2)}) %copy-start) | copy-done | bytes 262168
  2.4 0.0 copy-start.1
  2.4 1.0 %copy-done.1 = f32[1,256,512]{2,1,0:T(8,128)S(1)} copy-done((f32[1,256,512]{2,1,0:T(8,128)S(1)}, f32[1,256,512]{2,1,0:T(8,128)}, u32[]{:S(2)}) %copy-start.1) | copy-done | bytes 524312
  3.4 0.0 copy-start.2
  3.4 1.0 %copy-done.2 = f32[256,512]{1,0:T(8,128)S(1)} copy-done((f32[256,512]{1,0:T(8,128)S(1)}, f32[256,512]{1,0:T(8,128)}, u32[]{:S(2)}) %copy-start.2) | copy-done | bytes 524312
  4.5 0.0 copy-start.3
  4.5 0.9 %copy-done.3 = f32[256,256]{1,0:T(8,128)S(1)} copy-done((f32[256,256]{1,0:T(8,128)S(1)}, f32[256,256]{1,0:T(8,128)}, u32[]{:S(2)}) %copy-start.3) | copy-done | bytes 262168
  5.4 58.9 %shard_map.94 = (f32[1,256,512]{2,1,0:T(8,128)S(1)}, f32[256,512]{1,0:T(8,128)S(1)}, bf16[256,8192]{1,0:T(8,128)(2,1)S(1)}) custom-call(bf16[1,1,256,8192]{3,2,1,0:T(8,128)(2,1)} %grad.1, f32[1,256,512]{2,1,0:T(8,128)S(1)} %copy-done.1, f32[256,512]{1,0:T(8,128)S(1)} %copy-done.2, s32[8,256]{1,0:T(8,128)S(1)} %pad.4.idx, f32[256,256]{1,0:T(8,128)S(1)} %copy-done, ...), custom_call_target="tpu_custom_call" | custom-call | flops 1006632960 | bytes 8388608 | tf_op jit(solution)/shard_map/pallas_call | solution.py:365
  64.3 0.8 %copy.13 = f32[1,256,512]{2,1,0:T(8,128)} copy(f32[1,256,512]{2,1,0:T(8,128)S(1)} %get-tuple-element.6) | data formatting | bytes 1048576
  65.1 0.8 %copy.14 = f32[256,512]{1,0:T(8,128)} copy(f32[256,512]{1,0:T(8,128)S(1)} %get-tuple-element.7) | data formatting | bytes 1048576
  65.9 2.0 %copy.15 = bf16[256,8192]{1,0:T(8,128)(2,1)} copy(bf16[256,8192]{1,0:T(8,128)(2,1)S(1)} %get-tuple-element.8) | data formatting | bytes 8388608
  (1 shorter events, 0.0 us)
Async XLA Ops:
  1.4 0.9 %copy-start = (f32[256,256]{1,0:T(8,128)S(1)}, f32[256,256]{1,0:T(8,128)}, u32[]{:S(2)}) copy-start(f32[256,256]{1,0:T(8,128)} %constant.6.clone.rt.ct) | copy-start | bytes 786436
  2.4 1.0 %copy-start.1 = (f32[1,256,512]{2,1,0:T(8,128)S(1)}, f32[1,256,512]{2,1,0:T(8,128)}, u32[]{:S(2)}) copy-start(f32[1,256,512]{2,1,0:T(8,128)} %mom.1) | copy-start | bytes 1572868
  3.4 1.0 %copy-start.2 = (f32[256,512]{1,0:T(8,128)S(1)}, f32[256,512]{1,0:T(8,128)}, u32[]{:S(2)}) copy-start(f32[256,512]{1,0:T(8,128)} %master.1) | copy-start | bytes 1572868
  4.5 0.9 %copy-start.3 = (f32[256,256]{1,0:T(8,128)S(1)}, f32[256,256]{1,0:T(8,128)}, u32[]{:S(2)}) copy-start(f32[256,256]{1,0:T(8,128)} %constant.7.clone.rtt) | copy-start | bytes 786436

commit v2 on v1

v2 whole, which is shorter than its diff:
```python
import functools

import jax
import jax.numpy as jnp
import numpy as np
from jax import lax
from jax.experimental import pallas as pl
from jax.experimental.pallas import tpu as pltpu
from jax.sharding import PartitionSpec as P

BLOCK = 64
LANES = 128
TOP = 32767.0

momentum_decay = 0.9
step_rate = 0.5

HI = lax.Precision.HIGHEST
MESH = pl.DeviceIdType.MESH
F32 = jnp.float32
BF16 = jnp.bfloat16


def cosine_table(side):
    freqs = np.arange(side, dtype=np.float64)[:, None]
    places = np.arange(side, dtype=np.float64)[None, :]
    table = np.cos(np.pi * (2.0 * places + 1.0) * freqs / (2.0 * side))
    weights = np.where(freqs == 0.0, np.sqrt(1.0 / side), np.sqrt(2.0 / side))
    return table * weights


def split3(x):
    high = x.astype(BF16)
    rest = x - high.astype(F32)
    mid = rest.astype(BF16)
    low = (rest - mid.astype(F32)).astype(BF16)
    return high, mid, low


def dot(a, b):
    return jnp.dot(a, b, precision=HI, preferred_element_type=F32)


def dot_nt(a, b, precision=None):
    return lax.dot_general(a, b, (((1,), (1,)), ((), ())), precision=precision, preferred_element_type=F32)


def kernel(n_group, n, width,
           grad, mom_hbm, master_hbm, idx_hbm, rt_hbm, rtt_hbm, ct_hbm,
           mom_out, master_out, params_out,
           mine, sib, sendq, recvq, sends, recvs, acc, dense, param, idx_raw, idx, pick_all,
           mom, master, rt, rtt, ct,
           mine_sem, raw_send, raw_recv, q_send, q_recv, s_send, s_recv,
           idx_send, idx_recv, pick_send, pick_recv, load_sem,
           own_sem, ag_send, ag_recv, fw_send, fw_recv, y_send, y_recv, fy_send, fy_recv):
    rows = master.shape[0]
    half = rows // 2
    quarter = half // 2
    lines = half // BLOCK
    steps = n // 2
    count = 2 * steps - 1
    across = width // BLOCK
    slots = idx.shape[2]
    per_block = slots // across
    paired = n_group % 2 == 0
    shared = half // 4 if paired else 0
    sub = (half - shared) // 2

    g = lax.axis_index("group")
    s = lax.axis_index("shard")
    core = lax.rem(s, 2)
    chip = s // 2
    odd = lax.rem(chip, 2)
    pos = (1 - odd) * (chip // 2) + odd * (n - 1 - chip // 2)
    parity = lax.rem(g, 2)
    partner = g + 1 - 2 * parity

    def chip_at(offset):
        place = lax.rem(pos + (offset % n), n)
        back = place // (n // 2)
        return (1 - back) * (2 * place) + back * (2 * (n - 1 - place) + 1)

    sibling = 2 * chip + (1 - core)
    beside = {1: 2 * chip_at(1) + core, -1: 2 * chip_at(-1) + core}

    def columns(shard):
        return pl.ds(pl.multiple_of(shard * width, LANES), width)

    def other_group(k):
        return lax.rem(g + k, n_group)

    def side(sign):
        return 0 if sign == 1 else 1

    barrier = pltpu.get_barrier_semaphore()
    for sign in (1, -1):
        pl.semaphore_signal(barrier, inc=1, device_id={"shard": beside[sign]}, device_id_type=MESH)
    pl.semaphore_signal(barrier, inc=1, device_id={"shard": sibling}, device_id_type=MESH)
    for k in range(1, n_group):
        pl.semaphore_signal(barrier, inc=1, device_id={"group": other_group(k)}, device_id_type=MESH)

    order = [steps]
    for t in range(1, steps):
        order += [steps - t, n - (steps - t)]
    order += [0]

    own_loads = {}
    for r in order:
        own_loads[r] = pltpu.make_async_copy(
            grad.at[0, 0, :, columns(2 * chip_at(r) + core)], mine.at[r], mine_sem.at[r])
        own_loads[r].start()
    operands = []
    for i, (there, here) in enumerate((
            (idx_hbm, idx_raw.at[0]), (mom_hbm.at[0], mom), (rt_hbm, rt), (ct_hbm, ct),
            (rtt_hbm, rtt), (master_hbm, master))):
        copy = pltpu.make_async_copy(there, here, load_sem.at[i])
        copy.start()
        operands.append(copy)

    pl.semaphore_wait(barrier, 3 + n_group - 1)

    raw = {}
    for r in order:
        raw[r] = pltpu.make_async_remote_copy(
            src_ref=grad.at[0, 0, :, columns(2 * chip_at(r) + 1 - core)], dst_ref=sib.at[r],
            send_sem=raw_send.at[r], recv_sem=raw_recv.at[r],
            device_id={"shard": sibling}, device_id_type=MESH)
        raw[r].start()

    idx_copies = []
    for k in range(1, n_group):
        copy = pltpu.make_async_remote_copy(
            src_ref=idx_hbm, dst_ref=idx_raw.at[k],
            send_sem=idx_send.at[k - 1], recv_sem=idx_recv.at[k - 1],
            device_id={"group": other_group(k)}, device_id_type=MESH)
        copy.start()
        idx_copies.append(copy)

    def lay_indices(k):
        for a in range(rows // BLOCK):
            idx[k, a:a + 1, :] = jnp.concatenate(
                [idx_raw[k, a * across + b:a * across + b + 1, :] for b in range(across)], axis=1)

    def part_of(sign, first):
        return side(sign) if first else 1 - side(sign)

    ready = set()

    def arrived(r):
        if r not in ready:
            ready.add(r)
            own_loads[r].wait()
            raw[r].wait_recv()

    def q_copies(p, sign, m):
        d = 2 * p + side(sign)
        there = {"shard": beside[sign]}
        return (
            pltpu.make_async_remote_copy(
                src_ref=sendq.at[d, m], dst_ref=recvq.at[d, m],
                send_sem=q_send.at[d, m], recv_sem=q_recv.at[d, m],
                device_id=there, device_id_type=MESH),
            pltpu.make_async_remote_copy(
                src_ref=sends.at[d, m], dst_ref=recvs.at[d, m],
                send_sem=s_send.at[d, m], recv_sem=s_recv.at[d, m],
                device_id=there, device_id_type=MESH))

    def message(t, first):
        return 0 if t == 0 else 2 * t - 1 + (1 if first else 0)

    def received(d, m, lane):
        scale = recvs[d, m, 0:1, :]
        return recvq[d, m, :, pl.ds(lane * LANES, LANES)].astype(jnp.int32).astype(F32) * scale

    tiles = width // LANES

    def sum_step(p, t, first):
        for sign in (1, -1):
            d = 2 * p + side(sign)
            r = (sign * (steps - t)) % n
            m = message(t, first)
            arrived(r)
            has = t >= 2 or (t == 1 and first)
            if has:
                before = message(t - 1, first)
                for copy in q_copies(p, sign, before):
                    copy.wait_recv()
            band = pl.ds(p * half + part_of(sign, first) * quarter, quarter)
            values = []
            top = None
            for lane in range(tiles):
                cols = pl.ds(lane * LANES, LANES)
                x = mine[r, band, cols].astype(F32) + sib[r, band, cols].astype(F32)
                if has:
                    x = x + received(d, before, lane)
                values.append(x)
                peak = jnp.max(jnp.abs(x), axis=0, keepdims=True)
                top = peak if top is None else jnp.maximum(top, peak)
            top = jnp.maximum(top, 1e-30)
            inverse = TOP / top
            for lane in range(tiles):
                q = jnp.round(values[lane] * inverse).astype(jnp.int32).astype(jnp.int16)
                sendq[d, m, :, pl.ds(lane * LANES, LANES)] = q
            sends[d, m] = jnp.broadcast_to(top * (1.0 / TOP), (8, LANES))
            for copy in q_copies(p, sign, m):
                copy.start()

    def sum_end(p):
        arrived(0)
        for first in (False, True):
            for sign in (1, -1):
                for copy in q_copies(p, sign, message(steps - 1, first)):
                    copy.wait_recv()
        for part in range(2):
            band = pl.ds(p * half + part * quarter, quarter)
            for lane in range(tiles):
                cols = pl.ds(lane * LANES, LANES)
                x = mine[0, band, cols].astype(F32) + sib[0, band, cols].astype(F32)
                for sign in (1, -1):
                    x = x + received(2 * p + side(sign), message(steps - 1, part == side(sign)), lane)
                acc[band, cols] = momentum_decay * mom[band, cols] + x

    span = ct.shape[0]
    lane_block = lax.broadcasted_iota(jnp.int32, (1, slots), 1) // per_block

    def row_hot(ids):
        return lax.broadcasted_iota(jnp.int32, (BLOCK, slots), 0) == (ids >> 6)

    def col_hot(ids):
        places = lane_block * BLOCK + (ids & (BLOCK - 1))
        return lax.broadcasted_iota(jnp.int32, (width, slots), 0) == places

    def spread(ids, picked):
        hot = jnp.where(row_hot(ids), picked, 0.0)
        cols = jnp.where(col_hot(ids), 1.0, 0.0).astype(BF16)
        high, mid, low = split3(hot)
        return dot_nt(high, cols) + (dot_nt(mid, cols) + dot_nt(low, cols))

    def pick_copy(p, k):
        return pltpu.make_async_remote_copy(
            src_ref=pick_all.at[0, p], dst_ref=pick_all.at[k, p],
            send_sem=pick_send.at[p, k - 1], recv_sem=pick_recv.at[p, k - 1],
            device_id={"group": other_group(k)}, device_id_type=MESH)

    def forward(p):
        stage = dot(rt[...], acc[pl.ds(p * half, half), :])
        pieces = []
        for tile in range(width // span):
            pieces.append(dot_nt(ct[...], stage[:, tile * span:(tile + 1) * span], HI))
        high, mid, low = split3(jnp.concatenate(pieces, axis=0))
        pick_all[0, p] = jnp.zeros(pick_all.shape[2:], F32)
        for a in range(lines):
            line = p * lines + a
            ids = idx[0, line:line + 1, :]
            hot = lax.broadcasted_iota(jnp.int32, (half, slots), 0) == (ids >> 6) + a * BLOCK
            hot = jnp.where(hot, 1.0, 0.0).astype(BF16)
            at_row = (jnp.dot(high, hot, preferred_element_type=F32)
                      + (jnp.dot(mid, hot, preferred_element_type=F32)
                         + jnp.dot(low, hot, preferred_element_type=F32)))
            pick_all[0, p, a:a + 1, :] = jnp.sum(jnp.where(col_hot(ids), at_row, 0.0), axis=0, keepdims=True)
        for k in range(1, n_group):
            pick_copy(p, k).start()
        for a in range(lines):
            line = p * lines + a
            dense[pl.ds(line * BLOCK, BLOCK), :] = spread(idx[0, line:line + 1, :], pick_all[0, p, a:a + 1, :])

    def back(field, tile):
        return dot(field[:, tile * span:(tile + 1) * span], ct[...])

    def update(p):
        for k in range(1, n_group):
            pick_copy(p, k).wait_recv()
        bands = []
        for a in range(lines):
            line = p * lines + a
            band = dense[pl.ds(line * BLOCK, BLOCK), :]
            for k in range(1, n_group):
                band = band + spread(idx[k, line:line + 1, :], pick_all[k, p, a:a + 1, :])
            bands.append(band)
        stage = dot(rtt[...], jnp.concatenate(bands, axis=0))
        here = pl.ds(p * half, half)
        for tile in range(width // span):
            cols = pl.ds(tile * span, span)
            new = master[here, cols] - step_rate * jnp.tanh(back(stage, tile))
            master_out[here, cols] = new
            param[here, cols] = new.astype(BF16)

    def momentum_half(p):
        here = pl.ds(p * half, half)
        stage = dot(rtt[...], dense[here, :])
        for tile in range(width // span):
            cols = pl.ds(tile * span, span)
            mom_out[0, here, cols] = acc[here, cols] - back(stage, tile)

    def place(offset):
        return columns(2 * chip_at(offset) + core)

    def ring_rows(p, part):
        return pl.ds(pl.multiple_of(p * half + parity * shared + part * sub, 16), sub)

    def ag_copy(p, sign, t, first):
        d = 2 * p + side(sign)
        m = number[(t, first)]
        band = ring_rows(p, part_of(sign, first))
        where = params_out.at[band, place(-sign * t)]
        return pltpu.make_async_remote_copy(
            src_ref=param.at[band, :] if t == 0 else where, dst_ref=where,
            send_sem=ag_send.at[d, m], recv_sem=ag_recv.at[d, m],
            device_id={"shard": beside[sign]}, device_id_type=MESH)

    def ag_arrival(p, sign, t, first):
        d = 2 * p + side(sign)
        m = number[(t, first)]
        where = params_out.at[ring_rows(p, part_of(sign, first)), place(-sign * (t + 1))]
        return pltpu.make_async_remote_copy(
            src_ref=where, dst_ref=where,
            send_sem=ag_send.at[d, m], recv_sem=ag_recv.at[d, m],
            device_id={"shard": beside[sign]}, device_id_type=MESH)

    def fw_copy(p, sign, t, first, c):
        d = 2 * p + side(sign)
        m = number[(t, first)]
        where = params_out.at[ring_rows(p, part_of(sign, first)), columns(2 * chip_at(-sign * (t + 1)) + c)]
        return pltpu.make_async_remote_copy(
            src_ref=where, dst_ref=where,
            send_sem=fw_send.at[d, m], recv_sem=fw_recv.at[d, m],
            device_id={"shard": sibling}, device_id_type=MESH)

    def y_number(sign, t):
        return 2 * (steps - 1) if t == steps - 1 else t + side(sign) * (steps - 1)

    def y_rows(p, which):
        return pl.ds(pl.multiple_of(p * half + which * (half - shared), 16), shared)

    def y_copy(p, sign, t, which):
        where = params_out.at[y_rows(p, which), place(-sign * (t + 1))]
        i = y_number(sign, t)
        return pltpu.make_async_remote_copy(
            src_ref=where, dst_ref=where,
            send_sem=y_send.at[p, i], recv_sem=y_recv.at[p, i],
            device_id={"group": partner}, device_id_type=MESH)

    def fy_copy(p, sign, t, c):
        where = params_out.at[y_rows(p, 1 - parity), columns(2 * chip_at(-sign * (t + 1)) + c)]
        i = y_number(sign, t)
        return pltpu.make_async_remote_copy(
            src_ref=where, dst_ref=where,
            send_sem=fy_send.at[p, i], recv_sem=fy_recv.at[p, i],
            device_id={"shard": sibling}, device_id_type=MESH)

    trips = [(t, first) for t in range(steps) for first in ((True, False) if t < steps - 1 else (True,))]
    number = {trip: m for m, trip in enumerate(trips)}

    def own_copy(p):
        here = pl.ds(p * half, half)
        return pltpu.make_async_copy(param.at[here, :], params_out.at[here, place(0)], own_sem.at[p])

    def own_forward(p, c):
        here = pl.ds(p * half, half)
        return pltpu.make_async_remote_copy(
            src_ref=param.at[here, :], dst_ref=params_out.at[here, columns(2 * chip + c)],
            send_sem=fw_send.at[2 * p, count], recv_sem=fw_recv.at[2 * p, count],
            device_id={"shard": sibling}, device_id_type=MESH)

    sent = []
    pending = []
    y_done = []

    def go(p, sign, t, first):
        if (t, first) in number:
            copy = ag_copy(p, sign, t, first)
            copy.start()
            sent.append(copy)

    def gather_start(p):
        for first in (True, False):
            for sign in (1, -1):
                go(p, sign, 0, first)
        own_copy(p).start()
        own_forward(p, core).start()

    def y_take():
        p, sign, t = pending.pop(0)
        y_copy(p, sign, t, 1 - parity).wait_recv()
        fy_copy(p, sign, t, core).start()
        y_done.append((p, sign, t))

    def y_give(p, sign, t):
        if paired:
            y_copy(p, sign, t, parity).start()
            pending.append((p, sign, t))

    def gather_event(p, t, first):
        for sign in (1, -1):
            ag_arrival(p, sign, t, first).wait_recv()
            go(p, sign, t + 1, first)
            fw_copy(p, sign, t, first, core).start()
            if not first:
                y_give(p, sign, t)
        if t == steps - 1:
            y_give(p, 1, t)
        while len(pending) > 3:
            y_take()

    waves = [(0, True)]
    for t in range(1, steps):
        waves += [(t, False), (t, True)]
    sum_step(0, *waves[0])
    sum_step(0, *waves[1])
    for copy in operands:
        copy.wait()
    lay_indices(0)
    for wave in waves[2:]:
        sum_step(0, *wave)
    for wave in waves[:2]:
        sum_step(1, *wave)
    sum_end(0)
    forward(0)
    for wave in waves[2:-2]:
        sum_step(1, *wave)
    for k in range(1, n_group):
        idx_copies[k - 1].wait_recv()
        lay_indices(k)
    update(0)
    for wave in waves[-2:]:
        sum_step(1, *wave)
    gather_start(0)
    sum_end(1)
    forward(1)
    for trip in trips[:2]:
        gather_event(0, *trip)
    update(1)
    gather_start(1)
    momentum_half(0)
    left = trips[2:]
    others = list(trips)
    turn = 0
    while left or others:
        for trip in left[:2]:
            gather_event(0, *trip)
        left = left[2:]
        for trip in others[:2]:
            gather_event(1, *trip)
        others = others[2:]
        if turn == 0:
            momentum_half(1)
        turn += 1
    while pending:
        y_take()

    for p in range(2):
        for t, first in trips:
            for sign in (1, -1):
                fw_copy(p, sign, t, first, core).wait_send()
                fw_copy(p, sign, t, first, 1 - core).wait_recv()
        own_forward(p, core).wait_send()
        own_forward(p, 1 - core).wait_recv()
        own_copy(p).wait()
    for p, sign, t in y_done:
        y_copy(p, sign, t, parity).wait_send()
        fy_copy(p, sign, t, core).wait_send()
        fy_copy(p, sign, t, 1 - core).wait_recv()
    for copy in sent:
        copy.wait_send()
    for r in order:
        raw[r].wait_send()
    for p in range(2):
        for sign in (1, -1):
            for m in range(count):
                for copy in q_copies(p, sign, m):
                    copy.wait_send()
        for k in range(1, n_group):
            pick_copy(p, k).wait_send()
    for copy in idx_copies:
        copy.wait_send()


def local(n_group, n_shard, gradients, momentum, master, indices):
    rows, width = master.shape
    whole = gradients.shape[3]
    n = n_shard // 2
    steps = n // 2
    count = 2 * steps - 1
    height = rows // BLOCK
    slots = indices.shape[2] * indices.shape[3]
    idx = indices.reshape(-1, indices.shape[3])
    span = 256 if width % 256 == 0 else 128
    table = cosine_table(BLOCK)
    rt = np.kron(np.eye(height // 2), table).astype(np.float32)
    ct = np.kron(np.eye(span // BLOCK), table).astype(np.float32)
    others = max(n_group - 1, 1)
    dma = pltpu.SemaphoreType.DMA
    vmem = pl.BlockSpec(memory_space=pltpu.VMEM)
    hbm = pl.BlockSpec(memory_space=pltpu.HBM)
    free = pl.BlockSpec(memory_space=pl.ANY)
    body = functools.partial(kernel, n_group, n, width)
    return pl.pallas_call(
        body,
        out_shape=(
            jax.ShapeDtypeStruct((1, rows, width), F32),
            jax.ShapeDtypeStruct((rows, width), F32),
            jax.ShapeDtypeStruct((rows, whole), BF16),
        ),
        in_specs=[hbm] * 7,
        out_specs=(vmem, vmem, free),
        scratch_shapes=[
            pltpu.VMEM((n, rows, width), BF16),
            pltpu.VMEM((n, rows, width), BF16),
            pltpu.VMEM((4, count, rows // 4, width), jnp.int16),
            pltpu.VMEM((4, count, rows // 4, width), jnp.int16),
            pltpu.VMEM((4, count, 8, LANES), F32),
            pltpu.VMEM((4, count, 8, LANES), F32),
            pltpu.VMEM((rows, width), F32),
            pltpu.VMEM((rows, width), F32),
            pltpu.VMEM((rows, width), BF16),
            pltpu.VMEM((n_group,) + idx.shape, jnp.int32),
            pltpu.VMEM((n_group, -(-height // 8) * 8, slots), jnp.int32),
            pltpu.VMEM((n_group, 2, 8, slots), F32),
            pltpu.VMEM((rows, width), F32),
            pltpu.VMEM((rows, width), F32),
            pltpu.VMEM(rt.shape, F32),
            pltpu.VMEM(rt.shape, F32),
            pltpu.VMEM(ct.shape, F32),
            dma((n,)), dma((n,)), dma((n,)),
            dma((4, count)), dma((4, count)), dma((4, count)), dma((4, count)),
            dma((others,)), dma((others,)), dma((2, others)), dma((2, others)), dma((6,)),
            dma((2,)), dma((4, count)), dma((4, count)), dma((4, count + 1)), dma((4, count + 1)),
            dma((2, count)), dma((2, count)), dma((2, count)), dma((2, count)),
        ],
        compiler_params=pltpu.CompilerParams(
            collective_id=0, has_side_effects=True, vmem_limit_bytes=44 * 1024 * 1024),
        cost_estimate=pl.CostEstimate(
            flops=30 * rows * rows * width, bytes_accessed=4 * rows * whole, transcendentals=rows * width),
    )(gradients, momentum, master, idx, jnp.asarray(rt), jnp.asarray(rt.T.copy()), jnp.asarray(ct))


def solution(mesh):
    placed = (
        P("group", "shard", None, None),
        P("group", None, "shard"),
        P(None, "shard"),
        P("group", None, "shard", None),
    )
    return jax.shard_map(
        functools.partial(local, mesh.shape["group"], mesh.shape["shard"]),
        mesh=mesh,
        in_specs=placed,
        out_specs=(P("group", None, "shard"), P(None, "shard"), P()),
        check_vma=False,
    )
```

time: 68.2 us -> 71.6 us (1.050)
  Pallas kernels: 58.9 us -> 61.5 us
    pallas_call x1, Pallas kernels: 58.9 us -> 61.5 us  [local(): pl.pallas_call(body, out_shape=(jax.ShapeDtypeStruct((1, rows, width), F3...]
    unnamed x11 -> x15, local copies, waits for them, and re-layouts: 7.58 us -> 9.02 us
    another operation x1 -> x0, local copies, waits for them, and re-layouts: 0.8 us -> none  [local(): indices[0].reshape(height, slots)]
where the time goes in v2:
time: 71.6 us; the launch traced here: 71.2 us
  Pallas kernels  61.5 us (86%)
  local copies, waits for them, and re-layouts  9.02 us (13%)
    pallas_call x1, Pallas kernels, local(): pl.pallas_call(body, out_shape=(jax.ShapeDtypeStruct((1, rows, width), F3...  61.5 us
    unnamed x15, local copies, waits for them, and re-layouts  9.02 us

profile of v2, /device:TPU:0, one launch (start us, length us, event | category | flops | bytes accessed | tf_op | source)
XLA Modules:
  0.0 71.2 jit_solution(13518635242512050055)
XLA Ops:
  0.6 0.0 copy-start
  0.6 1.0 %copy-done = f32[1,256,512]{2,1,0:T(8,128)S(1)} copy-done((f32[1,256,512]{2,1,0:T(8,128)S(1)}, f32[1,256,512]{2,1,0:T(8,128)}, u32[]{:S(2)}) %copy-start) | copy-done | bytes 524312
  1.7 0.0 copy-start.1
  1.7 1.0 %copy-done.1 = f32[256,512]{1,0:T(8,128)S(1)} copy-done((f32[256,512]{1,0:T(8,128)S(1)}, f32[256,512]{1,0:T(8,128)}, u32[]{:S(2)}) %copy-start.1) | copy-done | bytes 524312
  2.7 0.0 copy-start.2
  2.7 0.9 %copy-done.2 = f32[256,256]{1,0:T(8,128)S(1)} copy-done((f32[256,256]{1,0:T(8,128)S(1)}, f32[256,256]{1,0:T(8,128)}, u32[]{:S(2)}) %copy-start.2) | copy-done | bytes 262168
  3.7 0.0 copy-start.3
  3.7 0.8 %copy-done.3 = f32[128,128]{1,0:T(8,128)S(1)} copy-done((f32[128,128]{1,0:T(8,128)S(1)}, f32[128,128]{1,0:T(8,128)}, u32[]{:S(2)}) %copy-start.3) | copy-done | bytes 65560
  4.5 0.0 copy-start.4
  4.5 0.8 %copy-done.4 = f32[128,128]{1,0:T(8,128)S(1)} copy-done((f32[128,128]{1,0:T(8,128)S(1)}, f32[128,128]{1,0:T(8,128)}, u32[]{:S(2)}) %copy-start.4) | copy-done | bytes 65560
  5.3 0.0 copy-start.5
  5.3 0.7 %copy-done.5 = s32[1,4,8,32]{3,2,1,0:T(8,128)S(1)} copy-done((s32[1,4,8,32]{3,2,1,0:T(8,128)S(1)}, s32[1,4,8,32]{3,2,1,0:T(8,128)}, u32[]{:S(2)}) %copy-start.5) | copy-done | bytes 4120
  6.1 61.5 %shard_map.94 = (f32[1,256,512]{2,1,0:T(8,128)S(1)}, f32[256,512]{1,0:T(8,128)S(1)}, bf16[256,8192]{1,0:T(8,128)(2,1)S(1)}) custom-call(bf16[1,1,256,8192]{3,2,1,0:T(8,128)(2,1)} %grad.1, f32[1,256,512]{2,1,0:T(8,128)S(1)} %copy-done, f32[256,512]{1,0:T(8,128)S(1)} %copy-done.1, s32[32,32]{1,0:T(8,128)S(1)} %bitcast.1, f32[128,128]{1,0:T(8,128)S(1)} %copy-done.4, ...), custom_call_target="tpu_custom_call" | custom-call | flops 1006632960 | bytes 8388608 | tf_op jit(solution)/shard_map/pallas_call | solution.py:497
  67.6 0.8 %copy.13 = f32[1,256,512]{2,1,0:T(8,128)} copy(f32[1,256,512]{2,1,0:T(8,128)S(1)} %get-tuple-element.6) | data formatting | bytes 1048576
  68.4 0.8 %copy.14 = f32[256,512]{1,0:T(8,128)} copy(f32[256,512]{1,0:T(8,128)S(1)} %get-tuple-element.7) | data formatting | bytes 1048576
  69.2 2.0 %copy.15 = bf16[256,8192]{1,0:T(8,128)(2,1)} copy(bf16[256,8192]{1,0:T(8,128)(2,1)S(1)} %get-tuple-element.8) | data formatting | bytes 8388608
Async XLA Ops:
  0.6 1.0 %copy-start = (f32[1,256,512]{2,1,0:T(8,128)S(1)}, f32[1,256,512]{2,1,0:T(8,128)}, u32[]{:S(2)}) copy-start(f32[1,256,512]{2,1,0:T(8,128)} %mom_hbm.1) | copy-start | bytes 1572868
  1.7 1.0 %copy-start.1 = (f32[256,512]{1,0:T(8,128)S(1)}, f32[256,512]{1,0:T(8,128)}, u32[]{:S(2)}) copy-start(f32[256,512]{1,0:T(8,128)} %master_hbm.1) | copy-start | bytes 1572868
  2.7 0.9 %copy-start.2 = (f32[256,256]{1,0:T(8,128)S(1)}, f32[256,256]{1,0:T(8,128)}, u32[]{:S(2)}) copy-start(f32[256,256]{1,0:T(8,128)} %constant.8.clone.ct_hbm) | copy-start | bytes 786436
  3.7 0.8 %copy-start.3 = (f32[128,128]{1,0:T(8,128)S(1)}, f32[128,128]{1,0:T(8,128)}, u32[]{:S(2)}) copy-start(f32[128,128]{1,0:T(8,128)} %constant.7.clone.rtt_hbm) | copy-start | bytes 196612
  4.5 0.8 %copy-start.4 = (f32[128,128]{1,0:T(8,128)S(1)}, f32[128,128]{1,0:T(8,128)}, u32[]{:S(2)}) copy-start(f32[128,128]{1,0:T(8,128)} %constant.6.clone.rt_hbm) | copy-start | bytes 196612
  5.3 0.7 %copy-start.5 = (s32[1,4,8,32]{3,2,1,0:T(8,128)S(1)}, s32[1,4,8,32]{3,2,1,0:T(8,128)}, u32[]{:S(2)}) copy-start(s32[1,4,8,32]{3,2,1,0:T(8,128)} %param.10) | copy-start | bytes 12292

commit v3 on v2

--- a/solution.py
+++ b/solution.py
@@ -62,7 +62,7 @@
     across = width // BLOCK
     slots = idx.shape[2]
     per_block = slots // across
-    paired = n_group % 2 == 0
+    paired = False
     shared = half // 4 if paired else 0
     sub = (half - shared) // 2
 
@@ -528,7 +528,7 @@
             dma((2, count)), dma((2, count)), dma((2, count)), dma((2, count)),
         ],
         compiler_params=pltpu.CompilerParams(
-            collective_id=0, has_side_effects=True, vmem_limit_bytes=44 * 1024 * 1024),
+            collective_id=0, has_side_effects=True, vmem_limit_bytes=58 * 1024 * 1024),
         cost_estimate=pl.CostEstimate(
             flops=30 * rows * rows * width, bytes_accessed=4 * rows * whole, transcendentals=rows * width),
     )(gradients, momentum, master, idx, jnp.asarray(rt), jnp.asarray(rt.T.copy()), jnp.asarray(ct))

time: 71.6 us -> 71.7 us (level)
  Pallas kernels: 61.5 us -> 62.5 us
    pallas_call x1, Pallas kernels: 61.5 us -> 62.5 us  [local(): pl.pallas_call(body, out_shape=(jax.ShapeDtypeStruct((1, rows, width), F3...]
    unnamed x15 -> x3, local copies, waits for them, and re-layouts: 9.02 us -> 8.37 us
where the time goes in v3:
time: 71.7 us; the launch traced here: 71.5 us
  Pallas kernels  62.5 us (87%)
  local copies, waits for them, and re-layouts  8.37 us (12%)
    pallas_call x1, Pallas kernels, local(): pl.pallas_call(body, out_shape=(jax.ShapeDtypeStruct((1, rows, width), F3...  62.5 us
    unnamed x3, local copies, waits for them, and re-layouts  8.37 us

profile of v3, /device:TPU:0, one launch (start us, length us, event | category | flops | bytes accessed | tf_op | source)
XLA Modules:
  0.0 71.5 jit_solution(3197462666845752963)
XLA Ops:
  0.6 62.5 %shard_map.94 = (f32[1,256,512]{2,1,0:T(8,128)}, f32[256,512]{1,0:T(8,128)}, bf16[256,8192]{1,0:T(8,128)(2,1)}) custom-call(bf16[1,1,256,8192]{3,2,1,0:T(8,128)(2,1)} %grad.1, f32[1,256,512]{2,1,0:T(8,128)} %mom_hbm.1, f32[256,512]{1,0:T(8,128)} %master_hbm.1, s32[32,32]{1,0:T(8,128)} %bitcast.1, f32[128,128]{1,0:T(8,128)} %constant.6.clone.rt_hbm, ...), custom_call_target="tpu_custom_call" | custom-call | flops 1006632960 | bytes 8388608 | tf_op jit(solution)/shard_map/pallas_call | solution.py:497
  63.1 1.9 %copy.13 = f32[1,256,512]{2,1,0:T(8,128)} copy(f32[1,256,512]{2,1,0:T(8,128)} %get-tuple-element.6) | data formatting | bytes 1048576
  65.0 1.9 %copy.14 = f32[256,512]{1,0:T(8,128)} copy(f32[256,512]{1,0:T(8,128)} %get-tuple-element.7) | data formatting | bytes 1048576
  66.8 4.6 %copy.15 = bf16[256,8192]{1,0:T(8,128)(2,1)} copy(bf16[256,8192]{1,0:T(8,128)(2,1)} %get-tuple-element.8) | data formatting | bytes 8388608
